TPU v7x, 32 devices: a whole 2x2x4 slice. The times are simulated.
32 devices in a mesh: row: 8 (over y, x, core), col: 4 (over z).
Axes of the slice: x: 2, y: 2, z: 4, core: 2. Of those that a mesh axis runs over, the one named last changes fastest.
Arguments:
- tiles: bfloat16 [2, 16384, 8192], P(None, 'row', 'col'), may hold values from -0.0625 to 0.0625
- probe: bfloat16 [2, 16384, 256], P(None, ('row', 'col')), may hold values from -6 to 6
- cluster_perm: int32 [2, 8, 2048], P(None, 'row'), may hold values from 0 to 2047, each once within a row
- tile_keep: int32 [2, 8, 4], P(None, 'row', 'col'), may hold values 0 or 1
Outputs:
- samples: float32 [2, 16384, 256], P(None, ('row', 'col'))
- leaf_basis: float32 [2, 16384, 256], P(None, ('row', 'col'))
Inputs may be any that keep to these rules, and one draw needn't show every extreme that they name: Each row of cluster_perm is a permutation. `tile_keep`: entries with c = 0 are not read.
All inputs are finite; a program needn't handle non-finite values. No bound on the sum of `tile_keep` on one device may be relied on, other than what follows from the above.
Results may differ from a plain program's by a relative error of at most 0.0003.
Values may be sent and summed in bfloat16 or wider, within the bound.
A program may use at most 128 MiB of HBM per device.

v0:
```python
import jax
import jax.numpy as jnp
from jax import lax
from jax.sharding import PartitionSpec as P


def passed_along(value, axis, steps):
    count = lax.axis_size(axis)
    pairs = [(source, (source + steps) % count) for source in range(count)]
    return lax.ppermute(value, axis, pairs)


def tile_terms(tile_block, probe_far, probe_near, weight):

    def compute(unused):
        forward = jnp.dot(tile_block, probe_far, preferred_element_type=jnp.float32)
        backward = lax.dot_general(
            tile_block, probe_near, (((0,), (0,)), ((), ())), preferred_element_type=jnp.float32
        )
        return (weight * forward, weight * backward)

    def skipped(unused):
        empty = jnp.zeros((tile_block.shape[1], probe_near.shape[1]), jnp.float32)
        return (empty, empty)

    return lax.cond(weight != 0.0, compute, skipped, None)


def orthogonal(block, factor):
    return jax.scipy.linalg.solve_triangular(factor, block.T, lower=True).T


def per_device(tiles, probe, cluster_perm, tile_keep):
    row_id = lax.axis_index("row")
    col_id = lax.axis_index("col")
    nrows = lax.axis_size("row")
    ncols = lax.axis_size("col")
    slots = tiles.shape[0]
    tile_len = tiles.shape[1]
    hops = (ncols - 1).bit_length()
    raw_rows = lax.all_gather(probe, "col", axis=1, tiled=True)
    omega = jnp.take_along_axis(raw_rows, cluster_perm[:, 0, :, None], axis=1)
    omega_far = omega
    for offset in range(1, ncols):
        moved = passed_along(omega, "row", -offset)
        moved = jnp.where(row_id + offset >= nrows, jnp.roll(moved, -1, axis=0), moved)
        omega_far = jnp.where(col_id == offset, moved, omega_far)
    keep_flags = tile_keep[:, 0, 0].astype(jnp.float32)
    forwards = []
    backwards = []
    for slot in range(slots):
        weight = jnp.where(col_id == 0, 0.5, keep_flags[slot])
        forward, backward = tile_terms(tiles[slot], omega_far[slot], omega[slot], weight)
        forwards.append(forward)
        backwards.append(backward)
    forward_total = jnp.stack(forwards, 0)
    backward_total = jnp.stack(backwards, 0)
    for bit in range(hops):
        step_len = 1 << bit
        moved = passed_along(backward_total, "row", step_len)
        moved = jnp.where(row_id - step_len < 0, jnp.roll(moved, 1, axis=0), moved)
        backward_total = jnp.where(col_id >> bit & 1 == 1, moved, backward_total)
    combined = forward_total + backward_total
    samples = lax.psum_scatter(combined, "col", scatter_dimension=1, tiled=True)
    local_gram = jnp.einsum("kip,kiq->kpq", samples, samples, precision=lax.Precision.HIGHEST)
    gram_sum = lax.psum(local_gram, "col")
    factor = jnp.linalg.cholesky(gram_sum / tile_len)
    leaf_basis = jax.vmap(orthogonal)(samples, factor)
    return (samples, leaf_basis)


def solution(mesh):
    placed = (
        P(None, "row", "col"),
        P(None, ("row", "col"), None),
        P(None, "row", None),
        P(None, "row", "col"),
    )
    return jax.shard_map(
        per_device,
        mesh=mesh,
        in_specs=placed,
        out_specs=(P(None, ("row", "col"), None), P(None, ("row", "col"), None)),
        check_vma=False,
    )
```

profile of v0, /device:TPU:0, one launch (start us, length us, event | category | flops | bytes accessed | tf_op | source)
XLA Modules:
  0.0 669.0 jit_solution(6031102521076126934)
XLA Ops:
  7.2 0.7 all-gather.2.cloned.1.call-update
  7.9 0.7 compare_and_fusion
  8.7 0.8 fusion.60
  9.5 48.8 %all-gather.2.cloned.1.call-done = bf16[2,2048,256]{2,1,0:T(8,128)(2,1)} async-done(((bf16[2,512,256]{2,1,0:T(8,128)(2,1)}), bf16[2,2048,256]{2,1,0:T(8,128)(2,1)}) %all-gather.2.cloned.1.call-update) | async-done | bytes 2097168 | tf_op jit(solution)/shard_map/all_gather | solution.py:41
  58.2 49.1 %gather_fusion = bf16[4096,256]{1,0:T(8,128)(2,1)S(1)} fusion(bf16[2,2048,256]{2,1,0:T(8,128)(2,1)} %all-gather.2.cloned.1.call-done, s32[4096]{0:T(1024)S(1)} %bitcast.94), kind=kCustom, calls=%fused_computation | custom fusion | bytes 4227072 | tf_op jit(solution)/shard_map/jit(take_along_axis)/gather | solution.py:42
  107.4 1.7 broadcast_select_fusion
  109.1 0.8 collective-permute-start
  109.9 1.5 collective-permute-start.1
  111.5 1.4 collective-permute-start.2
  112.9 0.6 fusion.67
  114.8 41.1 %collective-permute-done = bf16[2,2048,256]{2,1,0:T(8,128)(2,1)} collective-permute-done((bf16[2,2048,256]{2,1,0:T(8,128)(2,1)}, bf16[2,2048,256]{2,1,0:T(8,128)(2,1)}, u32[]{:S(2)}, u32[]{:S(2)}) %collective-permute-start) | collective-permute-done | bytes 2097184 | tf_op jit(solution)/shard_map/ppermute | solution.py:10
  155.9 1.7 fusion.66
  157.6 1.2 collective-permute-done.1
  158.8 1.7 fusion.65
  160.5 41.7 %collective-permute-done.2 = bf16[2,2048,256]{2,1,0:T(8,128)(2,1)} collective-permute-done((bf16[2,2048,256]{2,1,0:T(8,128)(2,1)}, bf16[2,2048,256]{2,1,0:T(8,128)(2,1)}, u32[]{:S(2)}, u32[]{:S(2)}) %collective-permute-start.2) | collective-permute-done | bytes 2097184 | tf_op jit(solution)/shard_map/ppermute | solution.py:10
  202.2 1.7 fusion.64
  203.9 4.0 fusion.46
  207.9 1.3 copy-done.3
  209.3 16.9 %conditional.2 = (f32[1,2048,256]{1,2,0:T(8,128)}, f32[1,2048,256]{1,2,0:T(8,128)S(1)}) conditional(s32[]{:T(128)} %convert_element_type.11, () %tuple.32, (f32[]{:T(128)}, bf16[2,2048,2048]{2,1,0:T(8,128)(2,1)}, bf16[2,2048,256]{2,1,0:T(8,128)(2,1)S(1)}, bf16[2,2048,256]{2,1,0:T(8,128)(2,1)}) %tuple.33), branch_computations={%region_0.0_spmd, %region_1.2_spmd} | conditional | flops 4296015872 | bytes 31458320 | solution.py:26
  209.3 5.7 fusion.9
  215.0 1.8 copy.40
  216.9 7.4 %fusion.15 = f32[1,2048,256]{2,1,0:T(8,128)} fusion(bf16[2,2048,2048]{2,1,0:T(8,128)(2,1)} %get-tuple-element.33, bf16[2,2048,256]{2,1,0:T(8,128)(2,1)} %get-tuple-element.35, f32[]{:T(128)} %get-tuple-element.32), kind=kOutput, calls=%fused_computation.10 | convolution fusion | flops 2148007936 | bytes 11534848 | tf_op jit(solution)/shard_map/cond/branch_1_fun/dot_general | solution.py:17
  224.3 1.9 copy.42
  226.2 1.5 constant_dynamic-update-slice_fusion.1
  227.7 17.2 %conditional.3 = (f32[1,2048,256]{1,2,0:T(8,128)}, f32[1,2048,256]{1,2,0:T(8,128)S(1)}) conditional(s32[]{:T(128)} %convert_element_type.12, () %tuple.34, (f32[]{:T(128)}, bf16[2,2048,2048]{2,1,0:T(8,128)(2,1)}, bf16[2,2048,256]{2,1,0:T(8,128)(2,1)}, bf16[2,2048,256]{2,1,0:T(8,128)(2,1)}) %tuple.84), branch_computations={%region_2.3_spmd, %region_3.4_spmd} | conditional | flops 4296015872 | bytes 31458320 | solution.py:26
  227.7 6.0 fusion.31
  233.7 1.8 copy.44
  235.5 7.5 %fusion.37 = f32[1,2048,256]{2,1,0:T(8,128)} fusion(bf16[2,2048,2048]{2,1,0:T(8,128)(2,1)} %get-tuple-element.37, bf16[2,2048,256]{2,1,0:T(8,128)(2,1)} %get-tuple-element.39, f32[]{:T(128)} %get-tuple-element.36), kind=kOutput, calls=%fused_computation.24 | convolution fusion | flops 2148007936 | bytes 11534848 | tf_op jit(solution)/shard_map/cond/branch_1_fun/dot_general | solution.py:17
  243.0 1.9 copy.46
  244.9 1.5 constant_dynamic-update-slice_fusion
  246.4 1.3 collective-permute-start.3
  247.6 70.5 %collective-permute-done.3 = f32[2,2048,256]{1,2,0:T(8,128)} collective-permute-done((f32[2,2048,256]{1,2,0:T(8,128)}, f32[2,2048,256]{1,2,0:T(8,128)}, u32[]{:S(2)}, u32[]{:S(2)}) %collective-permute-start.3) | collective-permute-done | bytes 4194336 | tf_op jit(solution)/shard_map/ppermute | solution.py:10
  318.1 2.6 fusion.63
  320.8 0.8 copy-done.1
  321.6 3.4 fusion.44
  325.0 5.1 collective-permute-start.4
  330.0 90.7 %collective-permute-done.4 = f32[2,2048,256]{1,2,0:T(8,128)} collective-permute-done((f32[2,2048,256]{1,2,0:T(8,128)}, f32[2,2048,256]{1,2,0:T(8,128)}, u32[]{:S(2)}, u32[]{:S(2)}) %collective-permute-start.4) | collective-permute-done | bytes 4194336 | tf_op jit(solution)/shard_map/ppermute | solution.py:10
  420.7 2.7 fusion.62
  423.4 5.7 maximum_add_fusion
  429.2 74.3 %reduce-scatter.2.cloned.1.call-done = f32[2,512,256]{1,2,0:T(8,128)} async-done(((f32[2,2048,256]{1,2,0:T(8,128)}), f32[2,512,256]{1,2,0:T(8,128)}) %reduce-scatter.2.cloned.1.call-update) | async-done | bytes 1048592 | tf_op jit(solution)/shard_map/reduce_scatter | solution.py:64
  503.5 3.6 fusion.68
  507.3 1.3 copy.32
  508.6 37.5 %all-reduce.3.cloned.1.call-done = f32[2,256,256]{1,2,0:T(8,128)} async-done(((f32[2,256,256]{1,2,0:T(8,128)}), f32[2,256,256]{1,2,0:T(8,128)}) %all-reduce.3.cloned.1.call-update) | async-done | bytes 524304 | tf_op jit(solution)/shard_map/psum | solution.py:66
  546.1 1.1 broadcast_multiply_fusion
  547.3 0.2 copy.26
  547.5 0.1 fusion.52
  547.6 23.7 %custom-call.17 = f32[2,128,128]{2,1,0:T(8,128)S(1)} custom-call(f32[2,128,128]{2,1,0:T(8,128)S(1)} %cholesky.122), custom_call_target="Cholesky" | custom-call | tf_op jit(solution)/shard_map/jit(cholesky)/cholesky | solution.py:67
  571.3 19.7 %custom-call.18 = f32[2,1,128,128]{2,3,1,0:T(8,128)S(1)} custom-call(f32[2,1,128,128]{3,2,1,0:T(8,128)S(1)} %select_bitcast_fusion), custom_call_target="InvertDiagBlocksLowerTriangular" | custom-call | tf_op jit(solution)/shard_map/jit(cholesky)/cholesky | solution.py:67
  591.0 0.3 constant_dynamic-update-slice_fusion.3
  591.3 0.4 convolution_subtract_fusion
  591.7 23.5 %custom-call.19 = f32[2,128,128]{2,1,0:T(8,128)S(1)} custom-call(f32[2,128,128]{2,1,0:T(8,128)S(1)} %convolution_subtract_fusion), custom_call_target="Cholesky" | custom-call | tf_op jit(solution)/shard_map/jit(cholesky)/cholesky | solution.py:67
  615.2 0.2 compare_reduce_fusion
  615.4 0.1 select_select_fusion
  615.6 4.0 while.1
  615.6 0.6 fusion.75
  616.2 1.4 bitcast_dynamic-update-slice_fusion.2
  617.6 0.6 fusion.75
  618.2 1.4 bitcast_dynamic-update-slice_fusion.2
  619.6 39.6 %custom-call.20 = f32[2,2,128,128]{2,3,1,0:T(8,128)S(1)} custom-call(f32[2,2,128,128]{3,2,1,0:T(8,128)S(1)} %bitcast.99), custom_call_target="InvertDiagBlocksLowerTriangular" | custom-call | tf_op jit(solution)/shard_map/vmap(jit(_solve_triangular))/triangular_solve | solution.py:30
  659.2 0.6 fusion.50
  659.8 0.6 fusion.53
  660.4 0.6 fusion.49
  661.0 0.1 maximum_bitcast_fusion
  661.1 1.3 copy.33
  (27 shorter events, 0.4 us)
Async XLA Ops:
  7.2 51.1 %all-gather.2.cloned.1.call-start = ((), (), s32[]{:S(2)}) async-start(), calls=%async_computation.1 | async-start | bytes 2621440 | tf_op jit(solution)/shard_map/all_gather | solution.py:41
  7.9 495.6 %reduce-scatter.2.cloned.1.call-start = ((), (), s32[]{:S(2)}) async-start(), calls=%async_computation.2 | async-start | bytes 5242880 | tf_op jit(solution)/shard_map/reduce_scatter | solution.py:64
  107.4 5.5 copy-start.4
  109.1 46.8 %collective-permute-start = (bf16[2,2048,256]{2,1,0:T(8,128)(2,1)}, bf16[2,2048,256]{2,1,0:T(8,128)(2,1)}, u32[]{:S(2)}, u32[]{:S(2)}) collective-permute-start(bf16[2,2048,256]{2,1,0:T(8,128)(2,1)} %broadcast_select_fusion), channel_id=1, source_target_pairs={{0,20},{4,24},{8,28},{12,0},{16,4},{20,8},{24,12},{28,16},{1,21},{... | collective-permute-start | bytes 6291464 | tf_op jit(solution)/shard_map/ppermute | solution.py:10
  109.9 48.9 %collective-permute-start.1 = (bf16[2,2048,256]{2,1,0:T(8,128)(2,1)}, bf16[2,2048,256]{2,1,0:T(8,128)(2,1)}, u32[]{:S(2)}, u32[]{:S(2)}) collective-permute-start(bf16[2,2048,256]{2,1,0:T(8,128)(2,1)} %broadcast_select_fusion), channel_id=1, source_target_pairs={{0,24},{4,28},{8,0},{12,4},{16,8},{20,12},{24,16},{28,20},{1,25},{... | collective-permute-start | bytes 6291464 | tf_op jit(solution)/shard_map/ppermute | solution.py:10
  111.5 90.7 %collective-permute-start.2 = (bf16[2,2048,256]{2,1,0:T(8,128)(2,1)}, bf16[2,2048,256]{2,1,0:T(8,128)(2,1)}, u32[]{:S(2)}, u32[]{:S(2)}) collective-permute-start(bf16[2,2048,256]{2,1,0:T(8,128)(2,1)} %broadcast_select_fusion), channel_id=1, source_target_pairs={{0,28},{4,0},{8,4},{12,8},{16,12},{20,16},{24,20},{28,24},{1,29},{... | collective-permute-start | bytes 6291464 | tf_op jit(solution)/shard_map/ppermute | solution.py:10
  207.9 1.4 copy-start.3
  246.4 71.7 %collective-permute-start.3 = (f32[2,2048,256]{1,2,0:T(8,128)}, f32[2,2048,256]{1,2,0:T(8,128)}, u32[]{:S(2)}, u32[]{:S(2)}) collective-permute-start(f32[2,2048,256]{1,2,0:T(8,128)} %constant_dynamic-update-slice_fusion), channel_id=1, source_target_pairs={{0,4},{4,8},{8,12},{12,16},{16,20},{20,24},{24,28},{28,0},{1,5},{5... | collective-permute-start | bytes 12582920 | tf_op jit(solution)/shard_map/ppermute | solution.py:10
  318.1 3.4 copy-start.1
  325.0 95.8 %collective-permute-start.4 = (f32[2,2048,256]{1,2,0:T(8,128)}, f32[2,2048,256]{1,2,0:T(8,128)}, u32[]{:S(2)}, u32[]{:S(2)}) collective-permute-start(f32[2,2048,256]{1,2,0:T(8,128)} %fusion.44), channel_id=1, source_target_pairs={{0,8},{4,12},{8,16},{12,20},{16,24},{20,28},{24,0},{28,4},{1,9},{5... | collective-permute-start | bytes 12582920 | tf_op jit(solution)/shard_map/ppermute | solution.py:10
  429.2 116.9 %all-reduce.3.cloned.1.call-start = ((), (), s32[]{:S(2)}) async-start(), calls=%async_computation.3 | async-start | bytes 1048576 | tf_op jit(solution)/shard_map/psum | solution.py:66
  503.5 3.8 copy-start
  546.1 1.4 copy-start.2
Sparse Core Ops, SparseCore 0:
  9.6 48.6 all-gather.1
  429.3 74.1 reduce-scatter.1
  507.3 38.7 all-reduce.2
where the time goes:
time: 670 us; the launch traced here: 669 us
  waiting for transfers between devices  407 us (61%)
  other arithmetic  124 us (19%)
  local copies, waits for them, and re-layouts  79.6 us (12%)
  matrix products  32.7 us (5%)
  between operations  15.3 us (2%)
  starting transfers between devices  10.2 us (2%)
    ppermute x5, waiting for transfers between devices, passed_along(): return lax.ppermute(value, axis, pairs)  245 us
    reduce_scatter x1, waiting for transfers between devices, per_device(): samples = lax.psum_scatter(combined, 'col', scatter_dimension=1, tiled=True)  74.3 us
    another operation x9, other arithmetic, per_device(): factor = jnp.linalg.cholesky(gram_sum / tile_len)  67.1 us
    gather x1, local copies, waits for them, and re-layouts, per_device(): omega = jnp.take_along_axis(raw_rows, cluster_perm[:, 0, :, None], axis=1)  49.1 us
    all_gather x1, waiting for transfers between devices, per_device(): raw_rows = lax.all_gather(probe, 'col', axis=1, tiled=True)  48.8 us
    another operation x4, other arithmetic, orthogonal(): return jax.scipy.linalg.solve_triangular(factor, block.T, lower=True).T  39.8 us
    psum x1, waiting for transfers between devices, per_device(): gram_sum = lax.psum(local_gram, 'col')  37.5 us
    dot_general x2, matrix products, compute(): lax.dot_general(tile_block, probe_near, (((0,), (0,)), ((), ())), preferr...  14.9 us
  transfers between devices with their start and end apart: 8, of which 8 were waited for; matrix products, arithmetic and copies ran while one was open for 1% of the time, Pallas kernels for 0%

commit v1 on v0

v1 whole, which is shorter than its diff:
```python
import functools

import jax
import jax.numpy as jnp
from jax import lax
from jax.experimental import pallas as pl
from jax.experimental.pallas import tpu as pltpu
from jax.sharding import PartitionSpec as P

HIGHEST = lax.Precision.HIGHEST
LIMIT = 56 * 1024 * 1024
STEP = 256
NB = 64
AB_T = (((1,), (1,)), ((), ()))
AT_B = (((0,), (0,)), ((), ()))


def sort_rows(raw_ref, perm_ref, out_ref, slot):
    rows = out_ref.shape[1]
    points = raw_ref.shape[1]

    def block(index, carry):
        at = pl.multiple_of(index * STEP, STEP)
        order = perm_ref[slot, :, pl.ds(at, STEP)]
        order = jnp.broadcast_to(order, (128, STEP)).T
        total = jnp.zeros((STEP, out_ref.shape[2]), jnp.float32)
        pieces = []
        for lane in range(0, points, 128):
            column = lax.broadcasted_iota(jnp.int32, (STEP, 128), 1) + lane
            pieces.append(jnp.where(order == column, 1.0, 0.0).astype(jnp.bfloat16))
        hot = jnp.concatenate(pieces, axis=1)
        total = jnp.dot(hot, raw_ref[slot], preferred_element_type=jnp.float32)
        out_ref[slot, pl.ds(at, STEP), :] = total.astype(out_ref.dtype)
        return carry

    lax.fori_loop(0, rows // STEP, block, 0)


def sort_kernel(raw_ref, perm_ref, out_ref):
    for slot in range(out_ref.shape[0]):
        sort_rows(raw_ref, perm_ref, out_ref, slot)


def encode(value):
    top = jnp.max(jnp.abs(value), axis=1, keepdims=True)
    scale = jnp.where(top > 0.0, top, 1.0) * (1.0 / 32766.0)
    code = jnp.round(value * (1.0 / scale)).astype(jnp.int32).astype(jnp.int16)
    return code, scale


def backward_kernel(weight_ref, tiles_ref, omega_ref, code_ref, scale_ref):
    slot = pl.program_id(0)
    weight = weight_ref[slot]
    omega_t = omega_ref[0].T

    def block(index, carry):
        at = pl.multiple_of(index * STEP, STEP)
        value = jnp.dot(omega_t, tiles_ref[0, :, pl.ds(at, STEP)], preferred_element_type=jnp.float32)
        code, scale = encode(value.T * weight)
        code_ref[0, pl.ds(at, STEP), :] = code
        scale_ref[0, :, pl.ds(at, STEP)] = jnp.broadcast_to(scale, (STEP, 128)).T[0:1]
        return carry

    lax.fori_loop(0, code_ref.shape[1] // STEP, block, 0)


def forward_kernel(weight_ref, tiles_ref, far_ref, code_ref, scale_ref, out_ref):
    slot = pl.program_id(0)
    weight = weight_ref[slot]

    def block(index, carry):
        at = pl.multiple_of(index * STEP, STEP)
        value = jnp.dot(tiles_ref[0, pl.ds(at, STEP), :], far_ref[0], preferred_element_type=jnp.float32)
        scale = jnp.broadcast_to(scale_ref[0, :, pl.ds(at, STEP)], (128, STEP)).T
        code = code_ref[0, pl.ds(at, STEP), :].astype(jnp.int32).astype(jnp.float32)
        other = jnp.concatenate([code[:, lane:lane + 128] * scale for lane in range(0, code.shape[1], 128)], axis=1)
        out_ref[0, pl.ds(at, STEP), :] = value * weight + other
        return carry

    lax.fori_loop(0, out_ref.shape[1] // STEP, block, 0)


def eliminate(squares):
    parts = NB // 8
    row_at = lax.broadcasted_iota(jnp.int32, (8, 128), 0)
    lane_at = lax.broadcasted_iota(jnp.int32, (8, 128), 1)
    work = [[square[8 * t:8 * t + 8, :] for t in range(parts)] for square in squares]
    unit = [[jnp.where(row_at + 8 * t == lane_at, 1.0, 0.0) for t in range(parts)] for _ in squares]
    for j in range(NB):
        top, row = j // 8, j % 8
        for b in range(len(squares)):
            left, right = work[b][top][row:row + 1, :], unit[b][top][row:row + 1, :]
            inverse = 1.0 / left[:, j:j + 1]
            left_scaled, right_scaled = left * inverse, right * inverse
            for t in range(top, parts):
                factor = work[b][t][:, j:j + 1]
                if t == top:
                    factor = jnp.where(row_at[:, :1] > row, factor, 0.0)
                work[b][t] = work[b][t] - factor * left_scaled
                unit[b][t] = unit[b][t] - factor * right_scaled
    inverses = []
    for b in range(len(squares)):
        scaled = []
        for t in range(parts):
            pivot = jnp.sum(jnp.where(row_at + 8 * t == lane_at, work[b][t], 0.0), axis=1, keepdims=True)
            scaled.append(unit[b][t] * lax.rsqrt(pivot))
        inverses.append(jnp.concatenate(scaled, axis=0)[:, :NB])
    return inverses


def invert_factors(gram_ref, unit_ref, inverse_ref):
    slots, size = gram_ref.shape[0], gram_ref.shape[1]
    row_at = lax.broadcasted_iota(jnp.int32, (size, size), 0)
    lane_at = lax.broadcasted_iota(jnp.int32, (size, size), 1)
    for k in range(slots):
        unit_ref[k] = jnp.where(row_at == lane_at, 1.0, 0.0)

    def panel(index, carry):
        inverses = eliminate([gram_ref[k, 0:NB, 0:128] for k in range(slots)])
        for k in range(slots):
            across = jnp.dot(inverses[k], gram_ref[k, 0:NB, :], precision=HIGHEST, preferred_element_type=jnp.float32)
            done = jnp.dot(inverses[k], unit_ref[k, 0:NB, :], precision=HIGHEST, preferred_element_type=jnp.float32)
            inverse_ref[k, pl.ds(pl.multiple_of(index * NB, NB), NB), :] = done
            across_t = across.T[NB:, :]
            less = jnp.dot(across_t, across, precision=HIGHEST, preferred_element_type=jnp.float32)
            gram_ref[k, 0:size - NB, :] = pltpu.roll(gram_ref[k, NB:, :] - less, size - NB, 1)
            less = jnp.dot(across_t, done, precision=HIGHEST, preferred_element_type=jnp.float32)
            unit_ref[k, 0:size - NB, :] = unit_ref[k, NB:, :] - less
        return carry

    lax.fori_loop(0, size // NB, panel, 0)


def basis_kernel(points, samples_ref, gram_ref, basis_ref, work_ref, unit_ref, inverse_ref):
    work_ref[...] = gram_ref[...] * (1.0 / points)
    invert_factors(work_ref, unit_ref, inverse_ref)
    for k in range(samples_ref.shape[0]):
        basis_ref[k] = lax.dot_general(
            samples_ref[k], inverse_ref[k], AB_T, precision=HIGHEST, preferred_element_type=jnp.float32
        )


def per_device(tiles, probe, cluster_perm, tile_keep):
    row_id = lax.axis_index("row")
    col_id = lax.axis_index("col")
    nrows = lax.axis_size("row")
    ncols = lax.axis_size("col")
    slots, points, _ = tiles.shape
    width = probe.shape[2]
    params = pltpu.CompilerParams(vmem_limit_bytes=LIMIT)
    whole = pl.BlockSpec(memory_space=pltpu.VMEM)
    scalar = pl.BlockSpec(memory_space=pltpu.SMEM)

    def slot_block(rows, cols):
        return pl.BlockSpec((1, rows, cols), lambda k: (k, 0, 0))

    def shifted(value, sign):
        pairs = [
            (r * ncols + c, (r + sign * c) % nrows * ncols + c) for r in range(nrows) for c in range(ncols)
        ]
        return lax.ppermute(value, ("row", "col"), pairs)

    weight = jnp.where(col_id == 0, 0.5, tile_keep[:, 0, 0].astype(jnp.float32))
    raw = lax.all_gather(probe, "col", axis=1, tiled=True)
    omega = pl.pallas_call(
        sort_kernel,
        out_shape=jax.ShapeDtypeStruct((slots, points, width), jnp.bfloat16),
        in_specs=[whole, whole],
        out_specs=whole,
        compiler_params=params,
        name="sort_rows",
    )(raw, cluster_perm)
    far = shifted(omega, -1)
    code, scale = pl.pallas_call(
        backward_kernel,
        grid=(slots,),
        out_shape=(
            jax.ShapeDtypeStruct((slots, points, width), jnp.int16),
            jax.ShapeDtypeStruct((slots, 1, points), jnp.float32),
        ),
        in_specs=[scalar, slot_block(points, points), slot_block(points, width)],
        out_specs=(slot_block(points, width), slot_block(1, points)),
        compiler_params=params,
        cost_estimate=pl.CostEstimate(flops=4 * points * points * width, bytes_accessed=2 * tiles.size, transcendentals=0),
        name="backward_products",
    )(weight, tiles, omega)
    code, scale = shifted(code, 1), shifted(scale, 1)
    take_far = (row_id + col_id >= nrows).astype(jnp.int32)
    take_near = (row_id < col_id).astype(jnp.int32)
    selects = jnp.stack([take_far, take_near])

    def far_block(k, sel):
        return ((k + sel[0]) % slots, 0, 0)

    def near_block(k, sel):
        return ((k + slots - sel[1]) % slots, 0, 0)

    def plain_block(k, sel):
        return (k, 0, 0)

    combined = pl.pallas_call(
        lambda sel, *refs: forward_kernel(*refs),
        grid_spec=pltpu.PrefetchScalarGridSpec(
            num_scalar_prefetch=1,
            grid=(slots,),
            in_specs=[
                scalar,
                pl.BlockSpec((1, points, points), plain_block),
                pl.BlockSpec((1, points, width), far_block),
                pl.BlockSpec((1, points, width), near_block),
                pl.BlockSpec((1, 1, points), near_block),
            ],
            out_specs=pl.BlockSpec((1, points, width), plain_block),
        ),
        out_shape=jax.ShapeDtypeStruct((slots, points, width), jnp.float32),
        compiler_params=params,
        cost_estimate=pl.CostEstimate(flops=4 * points * points * width, bytes_accessed=2 * tiles.size, transcendentals=0),
        name="forward_products",
    )(selects, weight, tiles, far, code, scale)
    samples = lax.psum_scatter(combined, "col", scatter_dimension=1, tiled=True)
    local_gram = jnp.einsum("kip,kiq->kpq", samples, samples, precision=HIGHEST)
    gram_sum = lax.psum(local_gram, "col")
    square = pltpu.VMEM((slots, width, width), jnp.float32)
    leaf_basis = pl.pallas_call(
        functools.partial(basis_kernel, points),
        out_shape=jax.ShapeDtypeStruct(samples.shape, jnp.float32),
        in_specs=[whole, whole],
        out_specs=whole,
        scratch_shapes=[square, square, square],
        compiler_params=params,
        name="leaf_basis",
    )(samples, gram_sum)
    return (samples, leaf_basis)


def solution(mesh):
    placed = (
        P(None, "row", "col"),
        P(None, ("row", "col"), None),
        P(None, "row", None),
        P(None, "row", "col"),
    )
    return jax.shard_map(
        per_device,
        mesh=mesh,
        in_specs=placed,
        out_specs=(P(None, ("row", "col"), None), P(None, ("row", "col"), None)),
        check_vma=False,
    )
```

time: 670 us -> 338 us (0.50)
  waiting for transfers between devices: 407 us -> 221 us
  other arithmetic: 124 us -> 1.88 us
  local copies, waits for them, and re-layouts: 79.6 us -> 1.33 us
  Pallas kernels: 0 us -> 72.8 us
  matrix products: 32.7 us -> 4.2 us
  starting transfers between devices: 10.2 us -> 20.8 us
    ppermute x5 -> x3, waiting for transfers between devices: 245 us -> 0.01 us  [shifted(): return lax.ppermute(value, ('row', 'col'), pairs)]
    another operation x13 -> x1, other arithmetic: 107 us -> 0.64 us  [per_device(): selects = jnp.stack([take_far, take_near])]
    pallas_call x0 -> x4, Pallas kernels: none -> 72.8 us  [the longest x1 32.8 us: per_device(): pl.pallas_call(functools.partial(basis_kernel, points), out_shape=jax.Sha...]
    reduce_scatter x1, waiting for transfers between devices: 74.3 us -> 133 us  [per_device(): samples = lax.psum_scatter(combined, 'col', scatter_dimension=1, tiled=True)]
    gather x1 -> x0, local copies, waits for them, and re-layouts: 49.1 us -> none  [per_device(): omega = jnp.take_along_axis(raw_rows, cluster_perm[:, 0, :, None], axis=1)]
    dot_general x5 -> x1, matrix products: 30.2 us -> 4.2 us  [per_device(): local_gram = jnp.einsum('kip,kiq->kpq', samples, samples, precision=HIGHEST)]
    slice x6 -> x0, local copies, waits for them, and re-layouts: 11 us -> none  [the longest x2 5.35 us: per_device(): moved = jnp.where(row_id - step_len < 0, jnp.roll(moved, 1, axis=0), moved)]
    ppermute x5 -> x3, starting transfers between devices: 10.1 us -> 20.7 us  [shifted(): return lax.ppermute(value, ('row', 'col'), pairs)]
  transfers between devices with their start and end apart: 8 -> 6, of which waited for: 8 -> 3; matrix products, arithmetic and copies ran while one was open for 1% -> 1% of each run, Pallas kernels for 0% -> 5%
where the time goes in v1:
time: 338 us; the launch traced here: 336 us
  waiting for transfers between devices  221 us (65%)
  Pallas kernels  72.8 us (22%)
  starting transfers between devices  20.8 us (6%)
  between operations  13.8 us (4%)
  matrix products  4.2 us (1%)
    reduce_scatter x1, waiting for transfers between devices, per_device(): samples = lax.psum_scatter(combined, 'col', scatter_dimension=1, tiled=True)  133 us
    all_gather x1, waiting for transfers between devices, per_device(): raw = lax.all_gather(probe, 'col', axis=1, tiled=True)  49.1 us
    psum x1, waiting for transfers between devices, per_device(): gram_sum = lax.psum(local_gram, 'col')  39 us
    pallas_call x1, Pallas kernels, per_device(): pl.pallas_call(functools.partial(basis_kernel, points), out_shape=jax.Sha...  32.8 us
    ppermute x3, starting transfers between devices, shifted(): return lax.ppermute(value, ('row', 'col'), pairs)  20.7 us
    pallas_call x1, Pallas kernels, per_device(): pl.pallas_call(backward_kernel, grid=(slots,), out_shape=(jax.ShapeDtypeS...  16.3 us
    pallas_call x1, Pallas kernels, per_device(): pl.pallas_call(lambda sel, *refs: forward_kernel(*refs), grid_spec=pltpu....  13.1 us
    pallas_call x1, Pallas kernels, per_device(): pl.pallas_call(sort_kernel, out_shape=jax.ShapeDtypeStruct((slots, points...  10.6 us
  transfers between devices with their start and end apart: 6, of which 3 were waited for; matrix products, arithmetic and copies ran while one was open for 1% of the time, Pallas kernels for 5%

profile of v1, /device:TPU:0, one launch (start us, length us, event | category | flops | bytes accessed | tf_op | source)
XLA Modules:
  0.0 336.1 jit_solution(15321332709978867451)
XLA Ops:
  7.2 0.0 all-gather.2.cloned.1.call-start
  7.2 0.7 all-gather.2.cloned.1.call-update
  7.9 0.0 reduce-scatter.2.cloned.1.call-start
  8.0 1.2 fusion.weight_ref.refs_0_
  9.2 49.1 %all-gather.2.cloned.1.call-done.raw_ref = bf16[2,2048,256]{2,1,0:T(8,128)(2,1)} async-done(((bf16[2,512,256]{2,1,0:T(8,128)(2,1)}), bf16[2,2048,256]{2,1,0:T(8,128)(2,1)}) %all-gather.2.cloned.1.call-update) | async-done | bytes 2097168 | tf_op jit(solution)/shard_map/all_gather | solution.py:164
  58.2 10.6 %sort_rows.1.omega_ref = bf16[2,2048,256]{2,1,0:T(8,128)(2,1)} custom-call(bf16[2,2048,256]{2,1,0:T(8,128)(2,1)} %all-gather.2.cloned.1.call-done.raw_ref, s32[2,1,2048]{2,1,0:T(1,128)} %perm_ref.1), custom_call_target="tpu_custom_call" | custom-call | tf_op jit(solution)/shard_map/sort_rows/pallas_call | solution.py:165
  68.9 2.2 collective-permute-start
  71.1 16.3 %backward_products.1 = (s16[2,2048,256]{2,1,0:T(8,128)(2,1)}, f32[2,1,2048]{2,1,0:T(1,128)}) custom-call(f32[2]{0:T(128)} %fusion.weight_ref.refs_0_, bf16[2,2048,2048]{2,1,0:T(8,128)(2,1)} %refs_1_.1, bf16[2,2048,256]{2,1,0:T(8,128)(2,1)} %sort_rows.1.omega_ref), custom_call_target="tpu_custom_call" | custom-call | flops 4294967296 | bytes 16777216 | tf_op jit(solution)/shard_map/backward_products/pallas_call | solution.py:174
  87.4 17.1 %collective-permute-start.1 = (s16[2,2048,256]{2,1,0:T(8,128)(2,1)}, s16[2,2048,256]{2,1,0:T(8,128)(2,1)}, u32[]{:S(2)}, u32[]{:S(2)}) collective-permute-start(s16[2,2048,256]{2,1,0:T(8,128)(2,1)} %get-tuple-element.4), channel_id=1, source_target_pairs={{0,0},{1,5},{2,10},{3,15},{4,4},{5,9},{6,14},{7,19},{8,8},{9,13},{... | collective-permute-start | bytes 6291464 | tf_op jit(solution)/shard_map/ppermute | solution.py:161
  104.5 1.4 collective-permute-start.2
  105.9 0.6 add_convert_fusion.sel
  106.5 0.0 collective-permute-done.2.refs_4_
  106.5 0.0 copy-start.1
  106.5 0.0 collective-permute-done.refs_2_
  106.5 0.0 copy-start
  106.5 0.0 collective-permute-done.1.refs_3_
  106.5 0.6 copy-done.1
  107.1 0.8 copy-done
  107.9 13.1 %forward_products.1 = f32[2,2048,256]{2,1,0:T(8,128)} custom-call(s32[2]{0:T(128)} %add_convert_fusion.sel, f32[2]{0:T(128)} %fusion.weight_ref.refs_0_, bf16[2,2048,2048]{2,1,0:T(8,128)(2,1)} %refs_1_.1, bf16[2,2048,256]{2,1,0:T(8,128)(2,1)} %copy-done, s16[2,2048,256]{2,1,0:T(8,128)(2,1)} %collective-permute-done.1.refs_3_, f32[2,1,2048]{2,1,0:T(1,128)} %copy-done.1), custom_call_target="tpu_custom_call" | custom-call | flops 4294967296 | bytes 16777216 | tf_op jit(solution)/shard_map/forward_products/pallas_call | solution.py:201
  121.0 0.0 reduce-scatter.2.cloned.1.call-update
  121.0 0.0 all-reduce.2.cloned.1.call-start
  121.0 132.6 %reduce-scatter.2.cloned.1.call-done.samples_ref = f32[2,512,256]{2,1,0:T(8,128)} async-done(((f32[2,2048,256]{2,1,0:T(8,128)}), f32[2,512,256]{2,1,0:T(8,128)}) %reduce-scatter.2.cloned.1.call-update) | async-done | bytes 1048592 | tf_op jit(solution)/shard_map/reduce_scatter | solution.py:220
  253.6 4.2 %fusion.1 = f32[2,256,256]{2,1,0:T(8,128)} fusion(f32[2,512,256]{2,1,0:T(8,128)} %reduce-scatter.2.cloned.1.call-done.samples_ref), kind=kOutput, calls=%fused_computation.3 | convolution fusion | flops 805306368 | bytes 1572864 | tf_op jit(solution)/shard_map/kip,kiq->kpq/dot_general | solution.py:221
  257.8 0.0 all-reduce.2.cloned.1.call-update
  257.8 39.0 %all-reduce.2.cloned.1.call-done.gram_ref = f32[2,256,256]{2,1,0:T(8,128)} async-done(((f32[2,256,256]{2,1,0:T(8,128)}), f32[2,256,256]{2,1,0:T(8,128)}) %all-reduce.2.cloned.1.call-update) | async-done | bytes 524304 | tf_op jit(solution)/shard_map/psum | solution.py:222
  296.8 32.8 %leaf_basis.1 = f32[2,512,256]{2,1,0:T(8,128)} custom-call(f32[2,512,256]{2,1,0:T(8,128)} %reduce-scatter.2.cloned.1.call-done.samples_ref, f32[2,256,256]{2,1,0:T(8,128)} %all-reduce.2.cloned.1.call-done.gram_ref), custom_call_target="tpu_custom_call" | custom-call | tf_op jit(solution)/shard_map/leaf_basis/pallas_call | solution.py:224
Async XLA Ops:
  7.2 51.1 %all-gather.2.cloned.1.call-start = ((), (), s32[]{:S(2)}) async-start(), calls=%async_computation.1 | async-start | bytes 2621440 | tf_op jit(solution)/shard_map/all_gather | solution.py:164
  7.9 245.7 %reduce-scatter.2.cloned.1.call-start = ((), (), s32[]{:S(2)}) async-start(), calls=%async_computation.2 | async-start | bytes 5242880 | tf_op jit(solution)/shard_map/reduce_scatter | solution.py:220
  68.9 37.7 %collective-permute-start = (bf16[2,2048,256]{2,1,0:T(8,128)(2,1)}, bf16[2,2048,256]{2,1,0:T(8,128)(2,1)S(1)}, u32[]{:S(2)}, u32[]{:S(2)}) collective-permute-start(bf16[2,2048,256]{2,1,0:T(8,128)(2,1)} %sort_rows.1.omega_ref), channel_id=1, source_target_pairs={{0,0},{1,29},{2,26},{3,23},{4,4},{5,1},{6,30},{7,27},{8,8},{9,5},{... | collective-permute-start | bytes 6291464 | tf_op jit(solution)/shard_map/ppermute | solution.py:161
  87.4 19.2 %collective-permute-start.1 = (s16[2,2048,256]{2,1,0:T(8,128)(2,1)}, s16[2,2048,256]{2,1,0:T(8,128)(2,1)}, u32[]{:S(2)}, u32[]{:S(2)}) collective-permute-start(s16[2,2048,256]{2,1,0:T(8,128)(2,1)} %get-tuple-element.4), channel_id=1, source_target_pairs={{0,0},{1,5},{2,10},{3,15},{4,4},{5,9},{6,14},{7,19},{8,8},{9,13},{... | collective-permute-start | bytes 6291464 | tf_op jit(solution)/shard_map/ppermute | solution.py:161
  104.5 2.0 collective-permute-start.2
  106.5 0.6 copy-start.1
  106.5 1.4 copy-start
  121.0 175.8 %all-reduce.2.cloned.1.call-start = ((), (), s32[]{:S(2)}) async-start(), calls=%async_computation.3 | async-start | bytes 1048576 | tf_op jit(solution)/shard_map/psum | solution.py:222
Sparse Core Ops, SparseCore 0:
  9.6 48.6 all-gather.1
  121.1 132.4 reduce-scatter.1
  257.9 38.7 all-reduce.1

commit v2 on v1

v2 whole, which is shorter than its diff:
```python
import functools

import jax
import jax.numpy as jnp
from jax import lax
from jax.experimental import pallas as pl
from jax.experimental.pallas import tpu as pltpu
from jax.sharding import PartitionSpec as P

HIGHEST = lax.Precision.HIGHEST
LIMIT = 56 * 1024 * 1024
STEP = 256
NB = 64
AB_T = (((1,), (1,)), ((), ()))
AT_B = (((0,), (0,)), ((), ()))


def sort_rows(raw_ref, perm_ref, out_ref, slot):
    rows, width = out_ref.shape[1:]
    parts, per = raw_ref.shape[1:3]

    def block(index, carry):
        at = pl.multiple_of(index * STEP, STEP)
        order = jnp.broadcast_to(perm_ref[slot, :, pl.ds(at, STEP)], (128, STEP)).T
        total = jnp.zeros((STEP, width), jnp.float32)
        for part in range(parts):
            pieces = []
            for lane in range(part * per, part * per + per, 128):
                column = lax.broadcasted_iota(jnp.int32, (STEP, 128), 1) + lane
                pieces.append(jnp.where(order == column, 1.0, 0.0).astype(jnp.bfloat16))
            hot = jnp.concatenate(pieces, axis=1)
            total = total + jnp.dot(hot, raw_ref[slot, part], preferred_element_type=jnp.float32)
        out_ref[slot, pl.ds(at, STEP), :] = total.astype(out_ref.dtype)
        return carry

    lax.fori_loop(0, rows // STEP, block, 0)


def encode(value):
    top = jnp.max(jnp.abs(value), axis=1, keepdims=True)
    scale = jnp.where(top > 0.0, top, 1.0) * (1.0 / 32766.0)
    code = jnp.round(value * (1.0 / scale)).astype(jnp.int32).astype(jnp.int16)
    return code, scale


def decode(code, scale):
    value = code.astype(jnp.int32).astype(jnp.float32)
    scale = jnp.broadcast_to(scale, (128, scale.shape[1])).T
    return jnp.concatenate([value[:, lane:lane + 128] * scale for lane in range(0, value.shape[1], 128)], axis=1)


def as_lanes(scale):
    return jnp.broadcast_to(scale, (scale.shape[0], 128)).T[0:1]


def samples_kernel(
    nrows, n, weight_ref, tiles_ref, probe_ref, perm_ref, samples_ref, gram_ref,
    tile, raw, omega, far, back_code, back_scale, near_code, near_scale,
    combined, code, scale, got_code, got_scale, part_gram, got_gram,
    tile_sem, hop_send, hop_recv, far_send, far_recv, back_send, back_recv, own_send, own_recv, gram_send, gram_recv,
):
    slots, points, width = omega.shape
    per = points // n
    half = width // 2
    row, me = lax.axis_index("row"), lax.axis_index("col")
    before, after = lax.rem(row + nrows - me, nrows), lax.rem(row + me, nrows)
    from_wrap = jnp.where(row < me, 1, 0)
    to_wrap = jnp.where(row + me >= nrows, 1, 0)
    others = [lax.rem(me + o, n) for o in range(1, n)]
    mesh_id = pl.DeviceIdType.MESH

    def remote(src, dst, send, recv, where):
        return pltpu.make_async_remote_copy(
            src_ref=src, dst_ref=dst, send_sem=send, recv_sem=recv, device_id=where, device_id_type=mesh_id
        )

    def tile_copy(k):
        return pltpu.make_async_copy(tiles_ref.at[k], tile.at[k], tile_sem.at[k])

    def inside(at):
        return (at >= 0) & (at < n)

    def hop(k, side, s, block):
        step = 1 - 2 * side
        to = jnp.where(inside(me + step), me + step, me - step)
        src = probe_ref.at[k] if s == 0 else raw.at[k, block]
        return remote(src, raw.at[k, block], hop_send.at[k, side, s], hop_recv.at[k, side, s], {"col": to})

    def relay(k, s):
        for side in range(2):
            step = 1 - 2 * side
            block = me - s * step

            @pl.when(inside(block))
            def _():
                hop(k, side, s - 1, block).wait_recv()

            if s < n - 1:

                @pl.when(inside(block) & inside(me + step))
                def _():
                    hop(k, side, s, block).start()

    def far_copy(k):
        slot = lax.rem(k - from_wrap + slots, slots)
        return remote(omega.at[k], far.at[slot], far_send.at[k], far_recv.at[slot], {"row": before})

    def far_wait(slot):
        remote(omega.at[slot], far.at[slot], far_send.at[slot], far_recv.at[slot], {"row": before}).wait_recv()

    def back_copies(k, slot):
        return (
            remote(back_code.at[k], near_code.at[slot], back_send.at[k, 0], back_recv.at[slot, 0], {"row": after}),
            remote(back_scale.at[k], near_scale.at[slot], back_send.at[k, 1], back_recv.at[slot, 1], {"row": after}),
        )

    def own_copies(k, o):
        to = others[o]
        return (
            remote(code.at[k, to], got_code.at[k, o], own_send.at[k, o, 0], own_recv.at[k, o, 0], {"col": to}),
            remote(scale.at[k, to], got_scale.at[k, o], own_send.at[k, o, 1], own_recv.at[k, o, 1], {"col": to}),
        )

    def gram_copy(k, o):
        return remote(part_gram.at[k], got_gram.at[k, o], gram_send.at[k, o], gram_recv.at[k, o], {"col": others[o]})

    def sort_and_send(k):
        sort_rows(raw, perm_ref, omega, k)

        @pl.when(me > 0)
        def _():
            far_copy(k).start()

    def backward(k):
        omega_t = omega[k].T

        def block(index, carry):
            at = pl.multiple_of(index * STEP, STEP)
            value = jnp.dot(omega_t, tile[k, :, pl.ds(at, STEP)], preferred_element_type=jnp.float32)
            coded, scales = encode(value.T * weight_ref[k])
            back_code[k, pl.ds(at, STEP), :] = coded
            back_scale[k, :, pl.ds(at, STEP)] = as_lanes(scales)
            return carry

        lax.fori_loop(0, points // STEP, block, 0)

        @pl.when(me > 0)
        def _():
            for copy in back_copies(k, lax.rem(k + to_wrap, slots)):
                copy.start()

    def forward(k):

        @pl.when(me > 0)
        def _():
            far_wait(k)

        @pl.when(me == 0)
        def _():
            far[k] = omega[k]

        def block(index, carry):
            at = pl.multiple_of(index * per, per)
            value = jnp.dot(tile[k, pl.ds(at, per), :], far[k], preferred_element_type=jnp.float32)
            combined[k, index] = value * weight_ref[k]
            return carry

        lax.fori_loop(0, n, block, 0)

    def combine(k):

        @pl.when(me > 0)
        def _():
            for copy in back_copies(k, k):
                copy.wait_recv()

        @pl.when(me == 0)
        def _():
            near_code[k] = back_code[k]
            near_scale[k] = back_scale[k]

        def block(index, carry):
            at = pl.multiple_of(index * per, per)
            value = combined[k, index] + decode(near_code[k, pl.ds(at, per), :], near_scale[k, :, pl.ds(at, per)])
            combined[k, index] = value
            coded, scales = encode(value)
            code[k, index] = coded
            scale[k, index] = as_lanes(scales)
            return carry

        lax.fori_loop(0, n, block, 0)
        for o in range(n - 1):
            for copy in own_copies(k, o):
                copy.start()

    def collect(k):
        total = combined[k, me]
        for o in range(n - 1):
            for copy in own_copies(k, o):
                copy.wait_recv()
            total = total + decode(got_code[k, o], got_scale[k, o])
        samples_ref[k] = total
        total_t = total.T
        upper = jnp.dot(total_t[:half], total, precision=HIGHEST, preferred_element_type=jnp.float32)
        lower = jnp.dot(total_t[half:], total[:, half:], precision=HIGHEST, preferred_element_type=jnp.float32)
        part_gram[k, 0:half] = upper[:, :half]
        part_gram[k, half:2 * half] = upper[:, half:]
        part_gram[k, 2 * half:3 * half] = lower
        for o in range(n - 1):
            gram_copy(k, o).start()

    def gather_gram(k):
        total = part_gram[k]
        for o in range(n - 1):
            gram_copy(k, o).wait_recv()
            total = total + got_gram[k, o]
        gram_ref[k, 0:half, 0:half] = total[0:half]
        gram_ref[k, 0:half, half:] = total[half:2 * half]
        gram_ref[k, half:, 0:half] = total[half:2 * half].T
        gram_ref[k, half:, half:] = total[2 * half:]

    barrier = pltpu.get_barrier_semaphore()
    for to in others:
        pl.semaphore_signal(barrier, inc=1, device_id={"col": to}, device_id_type=mesh_id)

    @pl.when(me > 0)
    def _():
        pl.semaphore_signal(barrier, inc=1, device_id={"row": before}, device_id_type=mesh_id)
        pl.semaphore_signal(barrier, inc=1, device_id={"row": after}, device_id_type=mesh_id)
        pl.semaphore_wait(barrier, n + 1)

    @pl.when(me == 0)
    def _():
        pl.semaphore_wait(barrier, n - 1)

    for k in range(slots):
        for side in range(2):

            @pl.when(inside(me + 1 - 2 * side))
            def _():
                hop(k, side, 0, me).start()

    for k in range(slots):
        tile_copy(k).start()
        raw[k, me] = probe_ref[k]
    for s in range(1, n):
        relay(0, s)
    for k in range(slots):
        if k + 1 < slots:
            relay(k + 1, 1)
        sort_and_send(k)
        if k + 1 < slots:
            for s in range(2, n - 1):
                relay(k + 1, s)
        tile_copy(k).wait()
        backward(k)
        if k + 1 < slots:
            relay(k + 1, n - 1)
    for k in range(slots):
        forward(k)
        combine(k)
    for k in range(slots):
        collect(k)
    for k in range(slots):
        gather_gram(k)

    for k in range(slots):
        for side in range(2):
            step = 1 - 2 * side
            for s in range(n - 1):

                @pl.when(inside(me - s * step) & inside(me + step))
                def _():
                    hop(k, side, s, me - s * step).wait_send()

        @pl.when(me > 0)
        def _():
            far_copy(k).wait_send()
            for copy in back_copies(k, lax.rem(k + to_wrap, slots)):
                copy.wait_send()

        for o in range(n - 1):
            for copy in own_copies(k, o):
                copy.wait_send()
            gram_copy(k, o).wait_send()


def eliminate(squares):
    parts = NB // 8
    row_at = lax.broadcasted_iota(jnp.int32, (8, 128), 0)
    lane_at = lax.broadcasted_iota(jnp.int32, (8, 128), 1)
    work = [[square[8 * t:8 * t + 8, :] for t in range(parts)] for square in squares]
    unit = [[jnp.where(row_at + 8 * t == lane_at, 1.0, 0.0) for t in range(parts)] for _ in squares]
    for j in range(NB):
        top, row = j // 8, j % 8
        for b in range(len(squares)):
            left, right = work[b][top][row:row + 1, :], unit[b][top][row:row + 1, :]
            inverse = 1.0 / left[:, j:j + 1]
            left_scaled, right_scaled = left * inverse, right * inverse
            for t in range(top, parts):
                factor = work[b][t][:, j:j + 1]
                if t == top:
                    factor = jnp.where(row_at[:, :1] > row, factor, 0.0)
                work[b][t] = work[b][t] - factor * left_scaled
                unit[b][t] = unit[b][t] - factor * right_scaled
    inverses = []
    for b in range(len(squares)):
        scaled = []
        for t in range(parts):
            pivot = jnp.sum(jnp.where(row_at + 8 * t == lane_at, work[b][t], 0.0), axis=1, keepdims=True)
            scaled.append(unit[b][t] * lax.rsqrt(pivot))
        inverses.append(jnp.concatenate(scaled, axis=0)[:, :NB])
    return inverses


def invert_factors(gram_ref, unit_ref, inverse_ref):
    slots, size = gram_ref.shape[0], gram_ref.shape[1]
    row_at = lax.broadcasted_iota(jnp.int32, (size, size), 0)
    lane_at = lax.broadcasted_iota(jnp.int32, (size, size), 1)
    for k in range(slots):
        unit_ref[k] = jnp.where(row_at == lane_at, 1.0, 0.0)

    def panel(index, carry):
        inverses = eliminate([gram_ref[k, 0:NB, 0:128] for k in range(slots)])
        for k in range(slots):
            across = jnp.dot(inverses[k], gram_ref[k, 0:NB, :], precision=HIGHEST, preferred_element_type=jnp.float32)
            done = jnp.dot(inverses[k], unit_ref[k, 0:NB, :], precision=HIGHEST, preferred_element_type=jnp.float32)
            inverse_ref[k, pl.ds(pl.multiple_of(index * NB, NB), NB), :] = done
            across_t = across.T[NB:, :]
            less = jnp.dot(across_t, across, precision=HIGHEST, preferred_element_type=jnp.float32)
            gram_ref[k, 0:size - NB, :] = pltpu.roll(gram_ref[k, NB:, :] - less, size - NB, 1)
            less = jnp.dot(across_t, done, precision=HIGHEST, preferred_element_type=jnp.float32)
            unit_ref[k, 0:size - NB, :] = unit_ref[k, NB:, :] - less
        return carry

    lax.fori_loop(0, size // NB, panel, 0)


def basis_kernel(points, samples_ref, gram_ref, basis_ref, work_ref, unit_ref, inverse_ref):
    work_ref[...] = gram_ref[...] * (1.0 / points)
    invert_factors(work_ref, unit_ref, inverse_ref)
    for k in range(samples_ref.shape[0]):
        basis_ref[k] = lax.dot_general(
            samples_ref[k], inverse_ref[k], AB_T, precision=HIGHEST, preferred_element_type=jnp.float32
        )


def per_device(tiles, probe, cluster_perm, tile_keep):
    nrows = lax.axis_size("row")
    ncols = lax.axis_size("col")
    slots, points, _ = tiles.shape
    per, width = probe.shape[1:]
    half = width // 2
    whole = pl.BlockSpec(memory_space=pltpu.VMEM)
    weight = jnp.where(lax.axis_index("col") == 0, 0.5, tile_keep[:, 0, 0].astype(jnp.float32))
    vmem = pltpu.VMEM
    sem = pltpu.SemaphoreType.DMA
    bf16, f32, i16 = jnp.bfloat16, jnp.float32, jnp.int16
    samples, gram_sum = pl.pallas_call(
        functools.partial(samples_kernel, nrows, ncols),
        out_shape=(
            jax.ShapeDtypeStruct((slots, per, width), f32),
            jax.ShapeDtypeStruct((slots, width, width), f32),
        ),
        in_specs=[pl.BlockSpec(memory_space=pltpu.SMEM), pl.BlockSpec(memory_space=pl.ANY), whole, whole],
        out_specs=(whole, whole),
        scratch_shapes=[
            vmem((slots, points, points), bf16),
            vmem((slots, ncols, per, width), bf16),
            vmem((slots, points, width), bf16),
            vmem((slots, points, width), bf16),
            vmem((slots, points, width), i16),
            vmem((slots, 1, points), f32),
            vmem((slots, points, width), i16),
            vmem((slots, 1, points), f32),
            vmem((slots, ncols, per, width), f32),
            vmem((slots, ncols, per, width), i16),
            vmem((slots, ncols, 1, per), f32),
            vmem((slots, ncols - 1, per, width), i16),
            vmem((slots, ncols - 1, 1, per), f32),
            vmem((slots, 3 * half, half), f32),
            vmem((slots, ncols - 1, 3 * half, half), f32),
            sem((slots,)),
            sem((slots, 2, ncols - 1)),
            sem((slots, 2, ncols - 1)),
            sem((slots,)),
            sem((slots,)),
            sem((slots, 2)),
            sem((slots, 2)),
            sem((slots, ncols - 1, 2)),
            sem((slots, ncols - 1, 2)),
            sem((slots, ncols - 1)),
            sem((slots, ncols - 1)),
        ],
        compiler_params=pltpu.CompilerParams(vmem_limit_bytes=LIMIT, collective_id=0, has_side_effects=True),
        cost_estimate=pl.CostEstimate(
            flops=12 * slots * points * points * width, bytes_accessed=2 * tiles.size, transcendentals=0
        ),
        name="samples",
    )(weight, tiles, probe, cluster_perm)
    square = vmem((slots, width, width), f32)
    leaf_basis = pl.pallas_call(
        functools.partial(basis_kernel, points),
        out_shape=jax.ShapeDtypeStruct(samples.shape, f32),
        in_specs=[whole, whole],
        out_specs=whole,
        scratch_shapes=[square, square, square],
        compiler_params=pltpu.CompilerParams(vmem_limit_bytes=LIMIT),
        name="leaf_basis",
    )(samples, gram_sum)
    return (samples, leaf_basis)


def solution(mesh):
    placed = (
        P(None, "row", "col"),
        P(None, ("row", "col"), None),
        P(None, "row", None),
        P(None, "row", "col"),
    )
    return jax.shard_map(
        per_device,
        mesh=mesh,
        in_specs=placed,
        out_specs=(P(None, ("row", "col"), None), P(None, ("row", "col"), None)),
        check_vma=False,
    )
```

time: 338 us -> 221 us (0.65)
  waiting for transfers between devices: 221 us -> 0 us
  Pallas kernels: 72.8 us -> 217 us
  starting transfers between devices: 20.8 us -> 0 us
  between operations: 13.8 us -> 0.64 us
  matrix products: 4.2 us -> 0 us
    pallas_call x3 -> x1, Pallas kernels: 40 us -> 184 us  [per_device(): pl.pallas_call(functools.partial(samples_kernel, nrows, ncols), out_shape...]
    reduce_scatter x1 -> x0, waiting for transfers between devices: 133 us -> none  [per_device(): samples = lax.psum_scatter(combined, 'col', scatter_dimension=1, tiled=True)]
    all_gather x1 -> x0, waiting for transfers between devices: 49.1 us -> none  [per_device(): raw = lax.all_gather(probe, 'col', axis=1, tiled=True)]
    psum x1 -> x0, waiting for transfers between devices: 39 us -> none  [per_device(): gram_sum = lax.psum(local_gram, 'col')]
    ppermute x3 -> x0, starting transfers between devices: 20.7 us -> none  [shifted(): return lax.ppermute(value, ('row', 'col'), pairs)]
    dot_general x1 -> x0, matrix products: 4.2 us -> none  [per_device(): local_gram = jnp.einsum('kip,kiq->kpq', samples, samples, precision=HIGHEST)]
  transfers between devices with their start and end apart: 6 -> 0, of which waited for: 3 -> 0; matrix products, arithmetic and copies ran while one was open for 1% -> 0% of each run, Pallas kernels for 5% -> 0%
where the time goes in v2:
time: 221 us
  Pallas kernels  217 us (98%)
  local copies, waits for them, and re-layouts  2.26 us (1%)
    pallas_call x1, Pallas kernels, per_device(): pl.pallas_call(functools.partial(samples_kernel, nrows, ncols), out_shape...  184 us
    pallas_call x1, Pallas kernels, per_device(): pl.pallas_call(functools.partial(basis_kernel, points), out_shape=jax.Sha...  32.8 us

profile of v2, /device:TPU:0, one launch (start us, length us, event | category | flops | bytes accessed | tf_op | source)
XLA Modules:
  0.0 221.2 jit_solution(1464149249953126878)
XLA Ops:
  0.6 1.2 fusion.weight_ref
  1.8 184.4 %samples.1 = (f32[2,512,256]{2,1,0:T(8,128)}, f32[2,256,256]{2,1,0:T(8,128)}) custom-call(f32[2]{0:T(128)} %fusion.weight_ref, bf16[2,2048,2048]{2,1,0:T(8,128)(2,1)} %tiles_ref.1, bf16[2,512,256]{2,1,0:T(8,128)(2,1)} %probe_ref.1, s32[2,1,2048]{2,1,0:T(1,128)} %perm_ref.1), custom_call_target="tpu_custom_call" | custom-call | flops 25769803776 | bytes 16777216 | tf_op jit(solution)/shard_map/samples/pallas_call | solution.py:359
  186.2 32.8 %leaf_basis.1 = f32[2,512,256]{2,1,0:T(8,128)} custom-call(f32[2,512,256]{2,1,0:T(8,128)} %get-tuple-element.8.samples_ref, f32[2,256,256]{2,1,0:T(8,128)} %get-tuple-element.5.gram_ref), custom_call_target="tpu_custom_call" | custom-call | tf_op jit(solution)/shard_map/leaf_basis/pallas_call | solution.py:402
  219.0 2.3 %copy.7 = f32[2,512,256]{2,1,0:T(8,128)} copy(f32[2,512,256]{2,1,0:T(8,128)} %get-tuple-element.8.samples_ref) | data formatting | bytes 2097152

commit v3 on v2

--- a/solution.py
+++ b/solution.py
@@ -57,7 +57,9 @@
     nrows, n, weight_ref, tiles_ref, probe_ref, perm_ref, samples_ref, gram_ref,
     tile, raw, omega, far, back_code, back_scale, near_code, near_scale,
     combined, code, scale, got_code, got_scale, part_gram, got_gram,
+    mid_code, mid_scale, last_code, last_scale,
     tile_sem, hop_send, hop_recv, far_send, far_recv, back_send, back_recv, own_send, own_recv, gram_send, gram_recv,
+    mid_send, mid_recv, last_send, last_recv,
 ):
     slots, points, width = omega.shape
     per = points // n
@@ -68,6 +70,8 @@
     to_wrap = jnp.where(row + me >= nrows, 1, 0)
     others = [lax.rem(me + o, n) for o in range(1, n)]
     mesh_id = pl.DeviceIdType.MESH
+    in_row = lax.rem(me, 2) == 1
+    evens = range(2, n, 2)
 
     def remote(src, dst, send, recv, where):
         return pltpu.make_async_remote_copy(
@@ -113,6 +117,45 @@
             remote(back_code.at[k], near_code.at[slot], back_send.at[k, 0], back_recv.at[slot, 0], {"row": after}),
             remote(back_scale.at[k], near_scale.at[slot], back_send.at[k, 1], back_recv.at[slot, 1], {"row": after}),
         )
+
+    def mid_copies(k, e, o):
+        to = others[o]
+        lanes = pl.ds(pl.multiple_of(to * per, per), per)
+        return (
+            remote(back_code.at[k, lanes], mid_code.at[k, e], mid_send.at[k, o, 0], mid_recv.at[k, e, 0], {"col": to}),
+            remote(
+                back_scale.at[k, :, lanes], mid_scale.at[k, e], mid_send.at[k, o, 1], mid_recv.at[k, e, 1], {"col": to}
+            ),
+        )
+
+    def last_copies(k, e, own):
+        offset = evens[e]
+        slot = lax.rem(k + jnp.where(row + offset >= nrows, 1, 0), slots)
+        lanes = pl.ds(pl.multiple_of(me * per, per), per)
+        sources = (back_code.at[k, lanes], back_scale.at[k, :, lanes]) if own else (mid_code.at[k, e], mid_scale.at[k, e])
+        targets = (last_code.at[slot, e], last_scale.at[slot, e])
+        to = {"row": lax.rem(row + offset, nrows)}
+        return [
+            remote(sources[i], targets[i], last_send.at[k, e, i], last_recv.at[slot, e, i], to) for i in range(2)
+        ]
+
+    def last_waits(slot, e):
+        to = {"row": lax.rem(row + evens[e], nrows)}
+        for i, buffer in enumerate((last_code, last_scale)):
+            remote(
+                mid_code.at[slot, e] if i == 0 else mid_scale.at[slot, e],
+                buffer.at[slot, e], last_send.at[slot, e, i], last_recv.at[slot, e, i], to,
+            ).wait_recv()
+
+    def pass_on(k):
+        for e, offset in enumerate(evens):
+
+            @pl.when(me != offset)
+            def _():
+                for copy in mid_copies(k, e, 0):
+                    copy.wait_recv()
+                for copy in last_copies(k, e, False):
+                    copy.start()
 
     def own_copies(k, o):
         to = others[o]
@@ -144,10 +187,20 @@
 
         lax.fori_loop(0, points // STEP, block, 0)
 
-        @pl.when(me > 0)
+        @pl.when(in_row)
         def _():
             for copy in back_copies(k, lax.rem(k + to_wrap, slots)):
                 copy.start()
+
+        for e, offset in enumerate(evens):
+
+            @pl.when(me == offset)
+            def _():
+                for o in range(n - 1):
+                    for copy in mid_copies(k, e, o):
+                        copy.start()
+                for copy in last_copies(k, e, True):
+                    copy.start()
 
     def forward(k):
 
@@ -169,7 +222,7 @@
 
     def combine(k):
 
-        @pl.when(me > 0)
+        @pl.when(in_row)
         def _():
             for copy in back_copies(k, k):
                 copy.wait_recv()
@@ -179,11 +232,19 @@
             near_code[k] = back_code[k]
             near_scale[k] = back_scale[k]
 
+        @pl.when(in_row | (me == 0))
+        def _():
+
+            def add(index, carry):
+                at = pl.multiple_of(index * per, per)
+                value = decode(near_code[k, pl.ds(at, per), :], near_scale[k, :, pl.ds(at, per)])
+                combined[k, index] = combined[k, index] + value
+                return carry
+
+            lax.fori_loop(0, n, add, 0)
+
         def block(index, carry):
-            at = pl.multiple_of(index * per, per)
-            value = combined[k, index] + decode(near_code[k, pl.ds(at, per), :], near_scale[k, :, pl.ds(at, per)])
-            combined[k, index] = value
-            coded, scales = encode(value)
+            coded, scales = encode(combined[k, index])
             code[k, index] = coded
             scale[k, index] = as_lanes(scales)
             return carry
@@ -195,6 +256,9 @@
 
     def collect(k):
         total = combined[k, me]
+        for e in range(len(evens)):
+            last_waits(k, e)
+            total = total + decode(last_code[k, e], last_scale[k, e])
         for o in range(n - 1):
             for copy in own_copies(k, o):
                 copy.wait_recv()
@@ -223,16 +287,9 @@
     for to in others:
         pl.semaphore_signal(barrier, inc=1, device_id={"col": to}, device_id_type=mesh_id)
 
-    @pl.when(me > 0)
-    def _():
-        pl.semaphore_signal(barrier, inc=1, device_id={"row": before}, device_id_type=mesh_id)
-        pl.semaphore_signal(barrier, inc=1, device_id={"row": after}, device_id_type=mesh_id)
-        pl.semaphore_wait(barrier, n + 1)
-
-    @pl.when(me == 0)
-    def _():
-        pl.semaphore_wait(barrier, n - 1)
-
+    for o in range(1, nrows):
+        pl.semaphore_signal(barrier, inc=1, device_id={"row": lax.rem(row + o, nrows)}, device_id_type=mesh_id)
+    pl.semaphore_wait(barrier, n + nrows - 2)
     for k in range(slots):
         for side in range(2):
 
@@ -257,6 +314,7 @@
         if k + 1 < slots:
             relay(k + 1, n - 1)
     for k in range(slots):
+        pass_on(k)
         forward(k)
         combine(k)
     for k in range(slots):
@@ -276,13 +334,33 @@
         @pl.when(me > 0)
         def _():
             far_copy(k).wait_send()
+
+        @pl.when(in_row)
+        def _():
             for copy in back_copies(k, lax.rem(k + to_wrap, slots)):
                 copy.wait_send()
+
+        for e, offset in enumerate(evens):
+            for copy in last_copies(k, e, False):
+                copy.wait_send()
+
+            @pl.when(me == offset)
+            def _():
+                for o in range(n - 1):
+                    for copy in mid_copies(k, e, o):
+                        copy.wait_send()
 
         for o in range(n - 1):
             for copy in own_copies(k, o):
                 copy.wait_send()
             gram_copy(k, o).wait_send()
+
+
+def reciprocal(value):
+    guess = pl.reciprocal(value, approx=True)
+    for _ in range(2):
+        guess = guess * (2.0 - value * guess)
+    return guess
 
 
 def eliminate(squares):
@@ -291,18 +369,24 @@
     lane_at = lax.broadcasted_iota(jnp.int32, (8, 128), 1)
     work = [[square[8 * t:8 * t + 8, :] for t in range(parts)] for square in squares]
     unit = [[jnp.where(row_at + 8 * t == lane_at, 1.0, 0.0) for t in range(parts)] for _ in squares]
-    for j in range(NB):
+    for j in range(0, NB, 2):
         top, row = j // 8, j % 8
         for b in range(len(squares)):
-            left, right = work[b][top][row:row + 1, :], unit[b][top][row:row + 1, :]
-            inverse = 1.0 / left[:, j:j + 1]
-            left_scaled, right_scaled = left * inverse, right * inverse
+            firsts = [jnp.broadcast_to(work[b][t][:, j:j + 1], (8, 128)) for t in range(top, parts)]
+            seconds = [jnp.broadcast_to(work[b][t][:, j + 1:j + 2], (8, 128)) for t in range(top, parts)]
+            head, cross, tail = firsts[0][row:row + 1], firsts[0][row + 1:row + 2], seconds[0][row + 1:row + 2]
+            inverse = reciprocal(head * tail - cross * cross)
+            ratio = cross * reciprocal(head)
+            tail, cross, head = tail * inverse, cross * inverse, head * inverse
+            pairs = [(array[b][top][row:row + 1], array[b][top][row + 1:row + 2]) for array in (work, unit)]
             for t in range(top, parts):
-                factor = work[b][t][:, j:j + 1]
+                one = firsts[t - top] * tail - seconds[t - top] * cross
+                two = seconds[t - top] * head - firsts[t - top] * cross
                 if t == top:
-                    factor = jnp.where(row_at[:, :1] > row, factor, 0.0)
-                work[b][t] = work[b][t] - factor * left_scaled
-                unit[b][t] = unit[b][t] - factor * right_scaled
+                    one = jnp.where(row_at > row + 1, one, jnp.where(row_at == row + 1, ratio, 0.0))
+                    two = jnp.where(row_at > row + 1, two, 0.0)
+                for array, (upper, lower) in zip((work, unit), pairs):
+                    array[b][t] = array[b][t] - (one * upper + two * lower)
     inverses = []
     for b in range(len(squares)):
         scaled = []
@@ -351,6 +435,7 @@
     slots, points, _ = tiles.shape
     per, width = probe.shape[1:]
     half = width // 2
+    evens = len(range(2, ncols, 2))
     whole = pl.BlockSpec(memory_space=pltpu.VMEM)
     weight = jnp.where(lax.axis_index("col") == 0, 0.5, tile_keep[:, 0, 0].astype(jnp.float32))
     vmem = pltpu.VMEM
@@ -380,6 +465,10 @@
             vmem((slots, ncols - 1, 1, per), f32),
             vmem((slots, 3 * half, half), f32),
             vmem((slots, ncols - 1, 3 * half, half), f32),
+            vmem((slots, evens, per, width), i16),
+            vmem((slots, evens, 1, per), f32),
+            vmem((slots, evens, per, width), i16),
+            vmem((slots, evens, 1, per), f32),
             sem((slots,)),
             sem((slots, 2, ncols - 1)),
             sem((slots, 2, ncols - 1)),
@@ -391,6 +480,10 @@
             sem((slots, ncols - 1, 2)),
             sem((slots, ncols - 1)),
             sem((slots, ncols - 1)),
+            sem((slots, ncols - 1, 2)),
+            sem((slots, evens, 2)),
+            sem((slots, evens, 2)),
+            sem((slots, evens, 2)),
         ],
         compiler_params=pltpu.CompilerParams(vmem_limit_bytes=LIMIT, collective_id=0, has_side_effects=True),
         cost_estimate=pl.CostEstimate(

time: 221 us -> 203 us (0.919)
  Pallas kernels: 217 us -> 198 us
    pallas_call x1, Pallas kernels: 184 us -> 174 us  [per_device(): pl.pallas_call(functools.partial(samples_kernel, nrows, ncols), out_shape...]
    pallas_call x1, Pallas kernels: 32.8 us -> 24.9 us  [per_device(): pl.pallas_call(functools.partial(basis_kernel, points), out_shape=jax.Sha...]
where the time goes in v3:
time: 203 us
  Pallas kernels  198 us (98%)
  local copies, waits for them, and re-layouts  2.26 us (1%)
    pallas_call x1, Pallas kernels, per_device(): pl.pallas_call(functools.partial(samples_kernel, nrows, ncols), out_shape...  174 us
    pallas_call x1, Pallas kernels, per_device(): pl.pallas_call(functools.partial(basis_kernel, points), out_shape=jax.Sha...  24.9 us

profile of v3, /device:TPU:0, one launch (start us, length us, event | category | flops | bytes accessed | tf_op | source)
XLA Modules:
  0.0 202.6 jit_solution(16071594471248005490)
XLA Ops:
  0.6 1.2 fusion.weight_ref
  1.8 173.6 %samples.1 = (f32[2,512,256]{2,1,0:T(8,128)}, f32[2,256,256]{2,1,0:T(8,128)}) custom-call(f32[2]{0:T(128)} %fusion.weight_ref, bf16[2,2048,2048]{2,1,0:T(8,128)(2,1)} %tiles_ref.1, bf16[2,512,256]{2,1,0:T(8,128)(2,1)} %probe_ref.1, s32[2,1,2048]{2,1,0:T(1,128)} %perm_ref.1), custom_call_target="tpu_custom_call" | custom-call | flops 25769803776 | bytes 16777216 | tf_op jit(solution)/shard_map/samples/pallas_call | solution.py:444
  175.4 24.9 %leaf_basis.1 = f32[2,512,256]{2,1,0:T(8,128)} custom-call(f32[2,512,256]{2,1,0:T(8,128)} %get-tuple-element.8.samples_ref, f32[2,256,256]{2,1,0:T(8,128)} %get-tuple-element.5.gram_ref), custom_call_target="tpu_custom_call" | custom-call | tf_op jit(solution)/shard_map/leaf_basis/pallas_call | solution.py:495
  200.3 2.3 %copy.7 = f32[2,512,256]{2,1,0:T(8,128)} copy(f32[2,512,256]{2,1,0:T(8,128)} %get-tuple-element.8.samples_ref) | data formatting | bytes 2097152

commit v4 on v3

--- a/solution.py
+++ b/solution.py
@@ -56,7 +56,7 @@
 def samples_kernel(
     nrows, n, weight_ref, tiles_ref, probe_ref, perm_ref, samples_ref, gram_ref,
     tile, raw, omega, far, back_code, back_scale, near_code, near_scale,
-    combined, code, scale, got_code, got_scale, part_gram, got_gram,
+    combined, code, scale, got_code, got_scale, part_gram, up_gram, got_gram, all_gram,
     mid_code, mid_scale, last_code, last_scale,
     tile_sem, hop_send, hop_recv, far_send, far_recv, back_send, back_recv, own_send, own_recv, gram_send, gram_recv,
     mid_send, mid_recv, last_send, last_recv,
@@ -157,15 +157,29 @@
                 for copy in last_copies(k, e, False):
                     copy.start()
 
-    def own_copies(k, o):
-        to = others[o]
+    def own_copies(k, side, block):
+        step = 1 - 2 * side
+        to = {"col": jnp.where(inside(me + step), me + step, me - step)}
         return (
-            remote(code.at[k, to], got_code.at[k, o], own_send.at[k, o, 0], own_recv.at[k, o, 0], {"col": to}),
-            remote(scale.at[k, to], got_scale.at[k, o], own_send.at[k, o, 1], own_recv.at[k, o, 1], {"col": to}),
+            remote(code.at[k, block], got_code.at[k, side, block], own_send.at[k, block, 0], own_recv.at[k, side, block, 0], to),
+            remote(scale.at[k, block], got_scale.at[k, side, block], own_send.at[k, block, 1], own_recv.at[k, side, block, 1], to),
         )
 
-    def gram_copy(k, o):
-        return remote(part_gram.at[k], got_gram.at[k, o], gram_send.at[k, o], gram_recv.at[k, o], {"col": others[o]})
+    middle = n // 2
+    inward = jnp.where(me < middle, 1, -1)
+    is_middle = (me == middle - 1) | (me == middle)
+    is_end = (me == 0) | (me == n - 1)
+    inner = {"col": me + inward}
+    outer = {"col": jnp.where(is_end, me + inward, me - inward)}
+
+    def gram_up(k):
+        return remote(part_gram.at[k], up_gram.at[k], gram_send.at[k, 0], gram_recv.at[k, 0], inner)
+
+    def gram_across(k):
+        return remote(part_gram.at[k], got_gram.at[k], gram_send.at[k, 0], gram_recv.at[k, 1], inner)
+
+    def gram_down(k):
+        return remote(all_gram.at[k], got_gram.at[k], gram_send.at[k, 1], gram_recv.at[k, 1], outer)
 
     def sort_and_send(k):
         sort_rows(raw, perm_ref, omega, k)
@@ -243,41 +257,77 @@
 
             lax.fori_loop(0, n, add, 0)
 
-        def block(index, carry):
-            coded, scales = encode(combined[k, index])
-            code[k, index] = coded
-            scale[k, index] = as_lanes(scales)
-            return carry
-
-        lax.fori_loop(0, n, block, 0)
-        for o in range(n - 1):
-            for copy in own_copies(k, o):
-                copy.start()
+        for i in range(n - 1):
+            for side, block in ((0, n - 1 - i), (1, i)):
+                sends = me < block if side == 0 else me > block
+                first = me == 0 if side == 0 else me == n - 1
+
+                @pl.when(sends & jnp.logical_not(first))
+                def _():
+                    for copy in own_copies(k, side, block):
+                        copy.wait_recv()
+                    combined[k, block] = combined[k, block] + decode(got_code[k, side, block], got_scale[k, side, block])
+
+                @pl.when(sends)
+                def _():
+                    coded, scales = encode(combined[k, block])
+                    code[k, block] = coded
+                    scale[k, block] = as_lanes(scales)
+                    for copy in own_copies(k, side, block):
+                        copy.start()
 
     def collect(k):
-        total = combined[k, me]
+        samples_ref[k] = combined[k, me]
         for e in range(len(evens)):
             last_waits(k, e)
-            total = total + decode(last_code[k, e], last_scale[k, e])
-        for o in range(n - 1):
-            for copy in own_copies(k, o):
-                copy.wait_recv()
-            total = total + decode(got_code[k, o], got_scale[k, o])
-        samples_ref[k] = total
+            samples_ref[k] = samples_ref[k] + decode(last_code[k, e], last_scale[k, e])
+        for side in range(2):
+
+            @pl.when(inside(me - 1 + 2 * side))
+            def _():
+                for copy in own_copies(k, side, me):
+                    copy.wait_recv()
+                samples_ref[k] = samples_ref[k] + decode(got_code[k, side, me], got_scale[k, side, me])
+
+        total = samples_ref[k]
         total_t = total.T
         upper = jnp.dot(total_t[:half], total, precision=HIGHEST, preferred_element_type=jnp.float32)
         lower = jnp.dot(total_t[half:], total[:, half:], precision=HIGHEST, preferred_element_type=jnp.float32)
         part_gram[k, 0:half] = upper[:, :half]
         part_gram[k, half:2 * half] = upper[:, half:]
         part_gram[k, 2 * half:3 * half] = lower
-        for o in range(n - 1):
-            gram_copy(k, o).start()
-
-    def gather_gram(k):
-        total = part_gram[k]
-        for o in range(n - 1):
-            gram_copy(k, o).wait_recv()
-            total = total + got_gram[k, o]
+
+    def sum_inward(k):
+
+        @pl.when(jnp.logical_not(is_end))
+        def _():
+            gram_up(k).wait_recv()
+            part_gram[k] = part_gram[k] + up_gram[k]
+
+        @pl.when(is_middle)
+        def _():
+            gram_across(k).start()
+
+        @pl.when(jnp.logical_not(is_middle))
+        def _():
+            gram_up(k).start()
+
+    def send_outward(k):
+        gram_across(k).wait_recv()
+
+        @pl.when(is_middle)
+        def _():
+            all_gram[k] = part_gram[k] + got_gram[k]
+
+        @pl.when(jnp.logical_not(is_middle))
+        def _():
+            all_gram[k] = got_gram[k]
+
+        @pl.when(jnp.logical_not(is_end))
+        def _():
+            gram_down(k).start()
+
+        total = all_gram[k]
         gram_ref[k, 0:half, 0:half] = total[0:half]
         gram_ref[k, 0:half, half:] = total[half:2 * half]
         gram_ref[k, half:, 0:half] = total[half:2 * half].T
@@ -313,14 +363,18 @@
         backward(k)
         if k + 1 < slots:
             relay(k + 1, n - 1)
-    for k in range(slots):
-        pass_on(k)
+    pass_on(0)
+    for k in range(slots):
         forward(k)
+        if k + 1 < slots:
+            pass_on(k + 1)
         combine(k)
     for k in range(slots):
         collect(k)
-    for k in range(slots):
-        gather_gram(k)
+        sum_inward(k)
+        if k > 0:
+            send_outward(k - 1)
+    send_outward(slots - 1)
 
     for k in range(slots):
         for side in range(2):
@@ -350,10 +404,19 @@
                     for copy in mid_copies(k, e, o):
                         copy.wait_send()
 
-        for o in range(n - 1):
-            for copy in own_copies(k, o):
-                copy.wait_send()
-            gram_copy(k, o).wait_send()
+        for side in range(2):
+            for block in range(n):
+
+                @pl.when(me < block if side == 0 else me > block)
+                def _():
+                    for copy in own_copies(k, side, block):
+                        copy.wait_send()
+
+        gram_across(k).wait_send()
+
+        @pl.when(jnp.logical_not(is_end))
+        def _():
+            gram_down(k).wait_send()
 
 
 def reciprocal(value):
@@ -461,10 +524,12 @@
             vmem((slots, ncols, per, width), f32),
             vmem((slots, ncols, per, width), i16),
             vmem((slots, ncols, 1, per), f32),
-            vmem((slots, ncols - 1, per, width), i16),
-            vmem((slots, ncols - 1, 1, per), f32),
+            vmem((slots, 2, ncols, per, width), i16),
+            vmem((slots, 2, ncols, 1, per), f32),
             vmem((slots, 3 * half, half), f32),
-            vmem((slots, ncols - 1, 3 * half, half), f32),
+            vmem((slots, 3 * half, half), f32),
+            vmem((slots, 3 * half, half), f32),
+            vmem((slots, 3 * half, half), f32),
             vmem((slots, evens, per, width), i16),
             vmem((slots, evens, 1, per), f32),
             vmem((slots, evens, per, width), i16),
@@ -476,10 +541,10 @@
             sem((slots,)),
             sem((slots, 2)),
             sem((slots, 2)),
-            sem((slots, ncols - 1, 2)),
-            sem((slots, ncols - 1, 2)),
-            sem((slots, ncols - 1)),
-            sem((slots, ncols - 1)),
+            sem((slots, ncols, 2)),
+            sem((slots, 2, ncols, 2)),
+            sem((slots, 2)),
+            sem((slots, 2)),
             sem((slots, ncols - 1, 2)),
             sem((slots, evens, 2)),
             sem((slots, evens, 2)),

time: 203 us -> 201 us (level)
  no operation moved by 1% of the time
where the time goes in v4:
time: 201 us
  Pallas kernels  197 us (98%)
  local copies, waits for them, and re-layouts  2.26 us (1%)
    pallas_call x1, Pallas kernels, per_device(): pl.pallas_call(functools.partial(samples_kernel, nrows, ncols), out_shape...  172 us
    pallas_call x1, Pallas kernels, per_device(): pl.pallas_call(functools.partial(basis_kernel, points), out_shape=jax.Sha...  24.9 us

profile of v4, /device:TPU:0, one launch (start us, length us, event | category | flops | bytes accessed | tf_op | source)
XLA Modules:
  0.0 201.3 jit_solution(9602332996119304750)
XLA Ops:
  0.6 1.2 fusion.weight_ref
  1.8 172.3 %samples.1 = (f32[2,512,256]{2,1,0:T(8,128)}, f32[2,256,256]{2,1,0:T(8,128)}) custom-call(f32[2]{0:T(128)} %fusion.weight_ref, bf16[2,2048,2048]{2,1,0:T(8,128)(2,1)} %tiles_ref.1, bf16[2,512,256]{2,1,0:T(8,128)(2,1)} %probe_ref.1, s32[2,1,2048]{2,1,0:T(1,128)} %perm_ref.1), custom_call_target="tpu_custom_call" | custom-call | flops 25769803776 | bytes 16777216 | tf_op jit(solution)/shard_map/samples/pallas_call | solution.py:507
  174.1 24.9 %leaf_basis.1 = f32[2,512,256]{2,1,0:T(8,128)} custom-call(f32[2,512,256]{2,1,0:T(8,128)} %get-tuple-element.8.samples_ref, f32[2,256,256]{2,1,0:T(8,128)} %get-tuple-element.5.gram_ref), custom_call_target="tpu_custom_call" | custom-call | tf_op jit(solution)/shard_map/leaf_basis/pallas_call | solution.py:560
  199.0 2.3 %copy.7 = f32[2,512,256]{2,1,0:T(8,128)} copy(f32[2,512,256]{2,1,0:T(8,128)} %get-tuple-element.8.samples_ref) | data formatting | bytes 2097152

commit v5 on v4

--- a/solution.py
+++ b/solution.py
@@ -70,8 +70,8 @@
     to_wrap = jnp.where(row + me >= nrows, 1, 0)
     others = [lax.rem(me + o, n) for o in range(1, n)]
     mesh_id = pl.DeviceIdType.MESH
-    in_row = lax.rem(me, 2) == 1
-    evens = range(2, n, 2)
+    in_row = me == 1
+    relayed = range(2, n)
 
     def remote(src, dst, send, recv, where):
         return pltpu.make_async_remote_copy(
@@ -129,7 +129,7 @@
         )
 
     def last_copies(k, e, own):
-        offset = evens[e]
+        offset = relayed[e]
         slot = lax.rem(k + jnp.where(row + offset >= nrows, 1, 0), slots)
         lanes = pl.ds(pl.multiple_of(me * per, per), per)
         sources = (back_code.at[k, lanes], back_scale.at[k, :, lanes]) if own else (mid_code.at[k, e], mid_scale.at[k, e])
@@ -140,7 +140,7 @@
         ]
 
     def last_waits(slot, e):
-        to = {"row": lax.rem(row + evens[e], nrows)}
+        to = {"row": lax.rem(row + relayed[e], nrows)}
         for i, buffer in enumerate((last_code, last_scale)):
             remote(
                 mid_code.at[slot, e] if i == 0 else mid_scale.at[slot, e],
@@ -148,7 +148,7 @@
             ).wait_recv()
 
     def pass_on(k):
-        for e, offset in enumerate(evens):
+        for e, offset in enumerate(relayed):
 
             @pl.when(me != offset)
             def _():
@@ -206,7 +206,7 @@
             for copy in back_copies(k, lax.rem(k + to_wrap, slots)):
                 copy.start()
 
-        for e, offset in enumerate(evens):
+        for e, offset in enumerate(relayed):
 
             @pl.when(me == offset)
             def _():
@@ -278,7 +278,7 @@
 
     def collect(k):
         samples_ref[k] = combined[k, me]
-        for e in range(len(evens)):
+        for e in range(len(relayed)):
             last_waits(k, e)
             samples_ref[k] = samples_ref[k] + decode(last_code[k, e], last_scale[k, e])
         for side in range(2):
@@ -394,7 +394,7 @@
             for copy in back_copies(k, lax.rem(k + to_wrap, slots)):
                 copy.wait_send()
 
-        for e, offset in enumerate(evens):
+        for e, offset in enumerate(relayed):
             for copy in last_copies(k, e, False):
                 copy.wait_send()
 
@@ -498,7 +498,7 @@
     slots, points, _ = tiles.shape
     per, width = probe.shape[1:]
     half = width // 2
-    evens = len(range(2, ncols, 2))
+    relayed = len(range(2, ncols))
     whole = pl.BlockSpec(memory_space=pltpu.VMEM)
     weight = jnp.where(lax.axis_index("col") == 0, 0.5, tile_keep[:, 0, 0].astype(jnp.float32))
     vmem = pltpu.VMEM
@@ -530,10 +530,10 @@
             vmem((slots, 3 * half, half), f32),
             vmem((slots, 3 * half, half), f32),
             vmem((slots, 3 * half, half), f32),
-            vmem((slots, evens, per, width), i16),
-            vmem((slots, evens, 1, per), f32),
-            vmem((slots, evens, per, width), i16),
-            vmem((slots, evens, 1, per), f32),
+            vmem((slots, relayed, per, width), i16),
+            vmem((slots, relayed, 1, per), f32),
+            vmem((slots, relayed, per, width), i16),
+            vmem((slots, relayed, 1, per), f32),
             sem((slots,)),
             sem((slots, 2, ncols - 1)),
             sem((slots, 2, ncols - 1)),
@@ -546,9 +546,9 @@
             sem((slots, 2)),
             sem((slots, 2)),
             sem((slots, ncols - 1, 2)),
-            sem((slots, evens, 2)),
-            sem((slots, evens, 2)),
-            sem((slots, evens, 2)),
+            sem((slots, relayed, 2)),
+            sem((slots, relayed, 2)),
+            sem((slots, relayed, 2)),
         ],
         compiler_params=pltpu.CompilerParams(vmem_limit_bytes=LIMIT, collective_id=0, has_side_effects=True),
         cost_estimate=pl.CostEstimate(

time: 201 us -> 177 us (0.88)
  the two profiles are of different devices: /device:TPU:0 before, /device:TPU:30 now
where the time goes in v5:
time: 177 us
  Pallas kernels  173 us (98%)
  local copies, waits for them, and re-layouts  2.26 us (1%)
    pallas_call x1, Pallas kernels, per_device(): pl.pallas_call(functools.partial(samples_kernel, nrows, ncols), out_shape...  148 us
    pallas_call x1, Pallas kernels, per_device(): pl.pallas_call(functools.partial(basis_kernel, points), out_shape=jax.Sha...  24.9 us

profile of v5, /device:TPU:30, one launch (start us, length us, event | category | flops | bytes accessed | tf_op | source)
XLA Modules:
  0.0 176.9 jit_solution(18307900778915458998)
XLA Ops:
  0.6 1.2 fusion.weight_ref
  1.8 147.9 %samples.1 = (f32[2,512,256]{2,1,0:T(8,128)}, f32[2,256,256]{2,1,0:T(8,128)}) custom-call(f32[2]{0:T(128)} %fusion.weight_ref, bf16[2,2048,2048]{2,1,0:T(8,128)(2,1)} %tiles_ref.1, bf16[2,512,256]{2,1,0:T(8,128)(2,1)} %probe_ref.1, s32[2,1,2048]{2,1,0:T(1,128)} %perm_ref.1), custom_call_target="tpu_custom_call" | custom-call | flops 25769803776 | bytes 16777216 | tf_op jit(solution)/shard_map/samples/pallas_call | solution.py:507
  149.7 24.9 %leaf_basis.1 = f32[2,512,256]{2,1,0:T(8,128)} custom-call(f32[2,512,256]{2,1,0:T(8,128)} %get-tuple-element.8.samples_ref, f32[2,256,256]{2,1,0:T(8,128)} %get-tuple-element.5.gram_ref), custom_call_target="tpu_custom_call" | custom-call | tf_op jit(solution)/shard_map/leaf_basis/pallas_call | solution.py:560
  174.7 2.3 %copy.7 = f32[2,512,256]{2,1,0:T(8,128)} copy(f32[2,512,256]{2,1,0:T(8,128)} %get-tuple-element.8.samples_ref) | data formatting | bytes 2097152
